TPU v7x, 32 devices: a whole 2x2x4 slice. The times are simulated.
32 devices in a mesh: grp: 1, mem: 32 (over z, y, x, core).
Axes of the slice: x: 2, y: 2, z: 4, core: 2. Of those that a mesh axis runs over, the one named last changes fastest.
Arguments:
- amplitudes: float32 [192, 1, 32, 2000], P('mem', 'grp'), may hold values from -6 to 6
- singles: float32 [250, 2000], replicated, may hold values from -5 to 5
- pair_list: int32 [192, 2], replicated, may hold values from 0 to 249, as said below
- mirror: int32 [192], replicated, may hold values from 0 to 191, as said below
- slab_rows: int32 [2048, 2], P('grp'), may hold values from 0 to 1999
- occ_energy: float32 [250], replicated, may hold values from -1 to -0.2
- vir_energy: float32 [2000], replicated, may hold values from 0.2 to 1
- integrals: float32 [2048, 1, 32, 2000], P('grp', None, 'mem'), may hold values from -0.0234375 to 0.0234375
Outputs:
- update: float32 [192, 2048], P('mem', 'grp')
Inputs may be any that keep to these rules, and one draw needn't show every extreme that they name: `pair_list`: each row holds two occupied orbitals i < j; no pair appears twice. mirror[mirror[p]] = p and mirror[p] != p; a pair p of owner block k = p // 6 is mapped into owner block (k + 32 / 2) mod 32.
All inputs are finite; a program needn't handle non-finite values.
Results may differ from a plain program's by a relative error of at most 0.000073.
Values sent between devices are 32-bit elements; how exact they have to be, the bound alone decides.
A program may use at most 128 MiB of HBM per device.

v0:
```python
import jax
import jax.numpy as jnp
from jax import lax
from jax.sharding import PartitionSpec as P


def body(amplitudes, singles, pair_list, mirror, slab_rows, occ_energy, vir_energy, integrals):
    owners = lax.axis_size("mem")
    member = lax.axis_index("mem")
    pair_dev = amplitudes.shape[0]
    pair_total = pair_dev * owners
    quarters = lax.all_gather(amplitudes, "grp", axis=1, tiled=True)
    regrouped = lax.all_to_all(quarters, "mem", split_axis=2, concat_axis=0, tiled=True)
    unpacked = regrouped - jnp.take(regrouped, mirror, axis=0)
    group_count = regrouped.shape[1]
    block_len = regrouped.shape[2]
    block_full = block_len * owners
    first_rows = jnp.take(singles, pair_list[:, 0], axis=0)
    second_rows = jnp.take(singles, pair_list[:, 1], axis=0)

    def window(orbital_rows):
        columns = orbital_rows[:, : group_count * block_full].reshape(
            pair_total, group_count, block_full
        )
        return lax.dynamic_slice_in_dim(columns, member * block_len, block_len, 2)

    first_window = window(first_rows)
    second_window = window(second_rows)
    tau_full = (
        unpacked
        + first_window[:, :, :, None] * second_rows[:, None, None, :]
        - second_window[:, :, :, None] * first_rows[:, None, None, :]
    )
    flat_tau = tau_full.reshape(pair_total, -1)
    flat_ints = integrals.reshape(integrals.shape[0], -1)
    summed = lax.psum_scatter(
        0.5
        * lax.dot_general(
            flat_tau,
            flat_ints,
            (((1,), (1,)), ((), ())),
            precision=lax.Precision.HIGHEST,
            preferred_element_type=jnp.float32,
        ),
        "mem",
        scatter_dimension=0,
        tiled=True,
    )
    own_pairs = lax.dynamic_slice_in_dim(pair_list, member * pair_dev, pair_dev, 0)
    occ_first = jnp.take(occ_energy, own_pairs[:, 0])
    occ_second = jnp.take(occ_energy, own_pairs[:, 1])
    vir_first = jnp.take(vir_energy, slab_rows[:, 0])
    vir_second = jnp.take(vir_energy, slab_rows[:, 1])
    denominator = (
        vir_first[None, :] + vir_second[None, :] - occ_first[:, None] - occ_second[:, None]
    )
    return summed / denominator


def solution(mesh):
    in_specs = (
        P("mem", "grp", None, None),
        P(),
        P(),
        P(),
        P("grp", None),
        P(),
        P(),
        P("grp", None, "mem", None),
    )
    out_specs = P("mem", "grp")
    return jax.shard_map(body, mesh=mesh, in_specs=in_specs, out_specs=out_specs, check_vma=False)
```

profile of v0, /device:TPU:0, one launch (start us, length us, event | category | flops | bytes accessed | tf_op | source)
XLA Modules:
  0.0 190.9 jit_solution(7629230299951570182)
XLA Ops:
  0.0 0.0 copy-start
  0.0 3.7 %copy.23 = f32[6,1,32,2000]{3,0,1,2:T(8,128)} copy(f32[6,1,32,2000]{3,2,1,0:T(8,128)} %param.14) | data formatting | bytes 3072000 | tf_op args[0]
  3.7 0.0 copy-start.6
  3.7 7.4 %all-to-all-start = ((f32[6,1,32,2000]{3,0,1,2:T(8,128)}), f32[6,1,32,2000]{3,0,1,2:T(8,128)}, u32[]{:S(2)}, u32[]{:S(2)}) async-start(f32[6,1,32,2000]{3,0,1,2:T(8,128)} %copy.23), calls=%async_computation | async-start | bytes 4194304 | tf_op jit(solution)/shard_map/all_to_all | solution.py:13
  11.1 0.0 copy-done.6
  11.2 1.9 %copy.26 = f32[250,2000]{1,0:T(8,128)S(1)} copy(f32[250,2000]{0,1:T(8,128)} %param.15) | data formatting | bytes 4000000 | tf_op args[1]
  13.1 2.3 %gather_fusion.2 = f32[192,2000]{1,0:T(8,128)} fusion(f32[250,2000]{1,0:T(8,128)S(1)} %copy.26, s32[1024]{0:T(1024)S(1)} %pad_clamp_fusion.2), kind=kCustom, calls=%fused_computation.3.clone | custom fusion | bytes 3072768 | tf_op jit(solution)/shard_map/jit(_take)/gather | solution.py:19
  15.5 1.6 broadcast_select_fusion
  17.1 0.0 copy-start.2
  17.1 1.2 copy-done.2
  18.3 2.3 %gather_fusion.1 = f32[192,2000]{1,0:T(8,128)} fusion(f32[250,2000]{1,0:T(8,128)S(1)} %copy.26, s32[1024]{0:T(1024)S(1)} %pad_clamp_fusion.3), kind=kCustom, calls=%fused_computation.clone | custom fusion | bytes 3072768 | tf_op jit(solution)/shard_map/jit(_take)/gather | solution.py:18
  20.6 0.0 copy-start.5
  20.6 1.6 broadcast_select_fusion.1
  22.2 0.0 copy-start.4
  22.2 0.0 copy-done.5
  22.3 0.0 copy-done
  22.3 11.8 %gather_fusion.4 = f32[2048]{0:T(1024)S(1)} fusion(f32[2000]{0:T(1024)S(1)} %copy-done, s32[2048]{0:T(1024)S(1)} %fusion.17), kind=kCustom, calls=%fused_computation.4.clone | custom fusion | bytes 24576 | tf_op jit(solution)/shard_map/jit(_take)/gather | solution.py:53
  34.1 0.0 copy-done.4
  34.1 0.0 slice-start
  34.1 0.0 copy-start.7
  34.1 11.8 %gather_fusion.3 = f32[2048]{0:T(1024)S(1)} fusion(f32[2000]{0:T(1024)S(1)} %copy-done, s32[2048]{0:T(1024)S(1)} %fusion.16), kind=kCustom, calls=%fused_computation.1.clone | custom fusion | bytes 24576 | tf_op jit(solution)/shard_map/jit(_take)/gather | solution.py:52
  45.9 0.2 dynamic-slice_reduce_fusion
  46.1 0.0 slice-done
  46.1 0.2 dynamic-slice_reduce_fusion.1
  46.3 0.1 constant_dynamic-slice_fusion
  46.4 0.0 copy-done.7
  46.4 13.6 %all-to-all-done = f32[6,1,32,2000]{3,0,1,2:T(8,128)} async-done(((f32[6,1,32,2000]{3,0,1,2:T(8,128)}), f32[6,1,32,2000]{3,0,1,2:T(8,128)}, u32[]{:S(2)}, u32[]{:S(2)}) %all-to-all-start) | async-done | bytes 1536032 | tf_op jit(solution)/shard_map/all_to_all | solution.py:13
  60.0 2.5 %copy.29 = f32[6,1,32,2000]{3,2,0,1:T(8,128)S(1)} copy(f32[6,1,32,2000]{3,0,1,2:T(8,128)} %all-to-all-done) | data formatting | bytes 3072000 | tf_op jit(solution)/shard_map/all_to_all | solution.py:13
  62.5 2.3 %copy.25 = f32[32,6,1,1,2000]{4,1,0,3,2:T(8,128)} copy(f32[32,6,1,1,2000]{4,0,1,3,2:T(8,128)S(1)} %bitcast.24) | data formatting | bytes 3072000 | tf_op jit(solution)/shard_map/all_to_all | solution.py:13
  64.8 1.6 all_to_all.18
  66.4 0.0 copy-start.3
  66.4 2.3 %gather_fusion = f32[192,2000]{1,0:T(8,128)} fusion(f32[192,2000]{1,0:T(8,128)S(1)} %all_to_all.18, s32[1024]{0:T(1024)S(1)} %pad_clamp_fusion.4), kind=kCustom, calls=%fused_computation.6 | custom fusion | bytes 3072768 | tf_op jit(solution)/shard_map/jit(_take)/gather | solution.py:14
  68.8 0.0 copy-done.3
  68.8 17.4 %fusion.3 = f32[192,2048]{1,0:T(8,128)} fusion(f32[2048,1,1,2000]{0,3,2,1:T(8,128)} %param.21, f32[192,2000]{1,0:T(8,128)} %copy-done.4, f32[192,2000]{1,0:T(8,128)S(1)} %copy-done.3, f32[192,2000]{1,0:T(8,128)S(1)} %all_to_all.18, f32[192,2000]{1,0:T(8,128)} %gather_fusion, f32[192]{0:T(256)S(1)} %dynamic-slice_reduce_fusion, ...), kind=kOutput, calls=%fused_computation.9 | convolution fusion | flops 9439881216 | bytes 24102592 | tf_op jit(solution)/shard_map/dot_general | solution.py:38
  86.2 0.0 copy-start.1
  86.2 80.8 %fusion = f32[8,2048]{1,0:T(8,128)S(1)} fusion(f32[192,2048]{1,0:T(8,128)} %fusion.3), kind=kCustom, calls=%all-reduce-scatter | all-reduce-scatter fusion | flops 524289 | bytes 1638400
  167.0 1.3 collective-permute-start
  168.3 1.3 collective-permute-start.1
  169.6 1.3 collective-permute-start.7
  170.9 0.0 copy-done.1
  170.9 0.6 gather_fusion.5
  171.6 0.6 gather_fusion.6
  172.2 1.3 collective-permute-start.2
  173.5 1.3 collective-permute-start.3
  174.8 0.0 collective-permute-done.7
  174.9 1.3 collective-permute-start.4
  176.2 0.0 collective-permute-done
  176.2 4.6 %collective-permute-start.5 = (f32[8,2048]{1,0:T(8,128)S(1)}, f32[8,2048]{1,0:T(8,128)S(1)}, u32[]{:S(2)}, u32[]{:S(2)}) collective-permute-start(f32[8,2048]{1,0:T(8,128)S(1)} %fusion), channel_id=1, source_target_pairs={{0,6},{1,7},{2,8},{3,9},{4,10},{5,11},{6,12},{7,13},{8,14},{9,15},... | collective-permute-start | bytes 196616
  180.8 0.0 collective-permute-done.1
  180.8 6.5 %collective-permute-start.6 = (f32[8,2048]{1,0:T(8,128)S(1)}, f32[8,2048]{1,0:T(8,128)S(1)}, u32[]{:S(2)}, u32[]{:S(2)}) collective-permute-start(f32[8,2048]{1,0:T(8,128)S(1)} %fusion), channel_id=1, source_target_pairs={{0,7},{1,8},{2,9},{3,10},{4,11},{5,12},{6,13},{7,14},{8,15},{9,16}... | collective-permute-start | bytes 196616
  187.3 0.0 collective-permute-done.2
  187.3 0.0 collective-permute-done.3
  187.3 0.0 collective-permute-done.4
  187.3 0.0 collective-permute-done.5
  187.3 1.8 collective-permute-done.6
  189.2 1.0 concatenate
  190.2 0.7 dynamic-slice_divide_fusion
  (17 shorter events, 0.1 us)
Async XLA Ops:
  0.0 22.3 %copy-start = (f32[2000]{0:T(1024)S(1)}, f32[2000]{0:T(1024)}, u32[]{:S(2)}) copy-start(f32[2000]{0:T(1024)} %param.20) | copy-start | bytes 24004
  3.7 7.4 %copy-start.6 = (s32[192,2]{0,1:T(2,128)S(1)}, s32[192,2]{0,1:T(2,128)}, u32[]{:S(2)}) copy-start(s32[192,2]{0,1:T(2,128)} %param.16) | copy-start | bytes 4612
  3.7 56.3 %all-to-all-start = ((f32[6,1,32,2000]{3,0,1,2:T(8,128)}), f32[6,1,32,2000]{3,0,1,2:T(8,128)}, u32[]{:S(2)}, u32[]{:S(2)}) async-start(f32[6,1,32,2000]{3,0,1,2:T(8,128)} %copy.23), calls=%async_computation | async-start | bytes 4194304 | tf_op jit(solution)/shard_map/all_to_all | solution.py:13
  17.1 1.2 copy-start.2
  20.6 1.6 copy-start.5
  22.2 11.9 %copy-start.4 = (f32[192,2000]{1,0:T(8,128)}, f32[192,2000]{1,0:T(8,128)S(1)}, u32[]{:S(2)}) copy-start(f32[192,2000]{1,0:T(8,128)S(1)} %broadcast_select_fusion.1) | copy-start | bytes 4608004
  34.1 12.0 %slice-start = ((f32[192,2000]{1,0:T(8,128)}), f32[192,32]{1,0:T(8,128)S(1)}, s32[]{:S(2)}) async-start(f32[192,2000]{1,0:T(8,128)} %copy-done.4), calls=%async_computation.1 | async-start | bytes 196608 | tf_op jit(solution)/shard_map/slice | solution.py:22
  34.1 12.3 %copy-start.7 = (s32[192]{0:T(256)S(1)}, s32[192]{0:T(256)}, u32[]{:S(2)}) copy-start(s32[192]{0:T(256)} %param.17) | copy-start | bytes 2308
  66.4 2.3 %copy-start.3 = (f32[192,2000]{1,0:T(8,128)S(1)}, f32[192,2000]{1,0:T(8,128)}, u32[]{:S(2)}) copy-start(f32[192,2000]{1,0:T(8,128)} %copy-done.2) | copy-start | bytes 4608004
  86.2 84.7 %copy-start.1 = (f32[250]{0:T(256)S(1)}, f32[250]{0:T(256)}, u32[]{:S(2)}) copy-start(f32[250]{0:T(256)} %param.19) | copy-start | bytes 3004
  167.0 9.1 %collective-permute-start = (f32[8,2048]{1,0:T(8,128)S(1)}, f32[8,2048]{1,0:T(8,128)S(1)}, u32[]{:S(2)}, u32[]{:S(2)}) collective-permute-start(f32[8,2048]{1,0:T(8,128)S(1)} %fusion), channel_id=1, source_target_pairs={{0,1},{1,2},{2,3},{3,4},{4,5},{5,6},{6,7},{7,8},{8,9},{9,10},{10,1... | collective-permute-start | bytes 196616
  168.3 12.5 %collective-permute-start.1 = (f32[8,2048]{1,0:T(8,128)S(1)}, f32[8,2048]{1,0:T(8,128)S(1)}, u32[]{:S(2)}, u32[]{:S(2)}) collective-permute-start(f32[8,2048]{1,0:T(8,128)S(1)} %fusion), channel_id=1, source_target_pairs={{0,2},{1,3},{2,4},{3,5},{4,6},{5,7},{6,8},{7,9},{8,10},{9,11},{10,... | collective-permute-start | bytes 196616
  169.6 5.2 %collective-permute-start.7 = (f32[6,2048]{1,0:T(8,128)S(1)}, f32[6,2048]{1,0:T(8,128)S(1)}, u32[]{:S(2)}, u32[]{:S(2)}) collective-permute-start(f32[6,2048]{1,0:T(8,128)S(1)} %slice.48), channel_id=1, source_target_pairs={{0,8},{1,9},{2,10},{3,11},{4,12},{5,13},{6,14},{7,15},{8,16},{9,17... | collective-permute-start | bytes 147464
  172.2 15.0 %collective-permute-start.2 = (f32[8,2048]{1,0:T(8,128)S(1)}, f32[8,2048]{1,0:T(8,128)S(1)}, u32[]{:S(2)}, u32[]{:S(2)}) collective-permute-start(f32[8,2048]{1,0:T(8,128)S(1)} %fusion), channel_id=1, source_target_pairs={{0,3},{1,4},{2,5},{3,6},{4,7},{5,8},{6,9},{7,10},{8,11},{9,12},{10... | collective-permute-start | bytes 196616
  173.5 13.8 %collective-permute-start.3 = (f32[8,2048]{1,0:T(8,128)S(1)}, f32[8,2048]{1,0:T(8,128)S(1)}, u32[]{:S(2)}, u32[]{:S(2)}) collective-permute-start(f32[8,2048]{1,0:T(8,128)S(1)} %fusion), channel_id=1, source_target_pairs={{0,4},{1,5},{2,6},{3,7},{4,8},{5,9},{6,10},{7,11},{8,12},{9,13},{1... | collective-permute-start | bytes 196616
  174.9 12.5 %collective-permute-start.4 = (f32[8,2048]{1,0:T(8,128)S(1)}, f32[8,2048]{1,0:T(8,128)S(1)}, u32[]{:S(2)}, u32[]{:S(2)}) collective-permute-start(f32[8,2048]{1,0:T(8,128)S(1)} %fusion), channel_id=1, source_target_pairs={{0,5},{1,6},{2,7},{3,8},{4,9},{5,10},{6,11},{7,12},{8,13},{9,14},{... | collective-permute-start | bytes 196616
  176.2 11.2 %collective-permute-start.5 = (f32[8,2048]{1,0:T(8,128)S(1)}, f32[8,2048]{1,0:T(8,128)S(1)}, u32[]{:S(2)}, u32[]{:S(2)}) collective-permute-start(f32[8,2048]{1,0:T(8,128)S(1)} %fusion), channel_id=1, source_target_pairs={{0,6},{1,7},{2,8},{3,9},{4,10},{5,11},{6,12},{7,13},{8,14},{9,15},... | collective-permute-start | bytes 196616
  180.8 8.4 %collective-permute-start.6 = (f32[8,2048]{1,0:T(8,128)S(1)}, f32[8,2048]{1,0:T(8,128)S(1)}, u32[]{:S(2)}, u32[]{:S(2)}) collective-permute-start(f32[8,2048]{1,0:T(8,128)S(1)} %fusion), channel_id=1, source_target_pairs={{0,7},{1,8},{2,9},{3,10},{4,11},{5,12},{6,13},{7,14},{8,15},{9,16}... | collective-permute-start | bytes 196616
where the time goes:
time: 192 us; the launch traced here: 191 us
  blocking collectives  80.8 us (42%)
  local copies, waits for them, and re-layouts  46.6 us (24%)
  starting transfers between devices  26.3 us (14%)
  matrix products  17.4 us (9%)
  waiting for transfers between devices  15.4 us (8%)
  other arithmetic  3.97 us (2%)
    unnamed x1, blocking collectives  80.8 us
    unnamed x8, starting transfers between devices  18.8 us
    dot_general x1, matrix products, body(): lax.dot_general(flat_tau, flat_ints, (((1,), (1,)), ((), ())), precision=...  17.4 us
    all_to_all x1, waiting for transfers between devices, body(): lax.all_to_all(quarters, 'mem', split_axis=2, concat_axis=0, tiled=True)  13.6 us
    gather x1, local copies, waits for them, and re-layouts, body(): vir_second = jnp.take(vir_energy, slab_rows[:, 1])  11.8 us
    gather x1, local copies, waits for them, and re-layouts, body(): vir_first = jnp.take(vir_energy, slab_rows[:, 0])  11.8 us
    unnamed x20, local copies, waits for them, and re-layouts  7.86 us
    all_to_all x1, starting transfers between devices, body(): lax.all_to_all(quarters, 'mem', split_axis=2, concat_axis=0, tiled=True)  7.43 us
  transfers between devices with their start and end apart: 9, of which 2 were waited for; matrix products, arithmetic and copies ran while one was open for 18% of the time, Pallas kernels for 0%

commit v1 on v0

--- a/solution.py
+++ b/solution.py
@@ -1,10 +1,392 @@
+import functools
+
 import jax
 import jax.numpy as jnp
 from jax import lax
+from jax.experimental import pallas as pl
+from jax.experimental.pallas import tpu as pltpu
 from jax.sharding import PartitionSpec as P
 
-
-def body(amplitudes, singles, pair_list, mirror, slab_rows, occ_energy, vir_energy, integrals):
+F32 = jnp.float32
+BF16 = jnp.bfloat16
+LANES = 128
+CHUNKS = 2
+COLUMN_BLOCKS = 4
+PLANE = 4
+CORES = 2
+
+
+def to(device):
+    return dict(device_id={"mem": device}, device_id_type=pl.DeviceIdType.MESH)
+
+
+def bf16_dot(left, right):
+    return jnp.dot(left, right, preferred_element_type=F32)
+
+
+def split_two(value):
+    high = value.astype(BF16)
+    return high, (value - high.astype(F32)).astype(BF16)
+
+
+def ladder_kernel(
+    n,
+    amp_ref,
+    mirror_ref,
+    pair_ref,
+    own_ref,
+    slab_ref,
+    occ_ref,
+    vir_ref,
+    singles_hbm,
+    ints_hbm,
+    out_ref,
+    send,
+    recv,
+    singles_ref,
+    ints_raw,
+    ints_high,
+    ints_low,
+    spart,
+    rows_ref,
+    partial,
+    got_core,
+    got_plane,
+    ready_depth,
+    got_depth,
+    denom_ref,
+    local_sem,
+    ints_sem,
+    a2a_send,
+    a2a_recv,
+    core_send,
+    core_recv,
+    plane_send,
+    plane_recv,
+    depth_send,
+    depth_recv,
+):
+    me = lax.axis_index("mem")
+    pair_dev, _, nc, nv = amp_ref.shape
+    pairs = pair_dev * n
+    depth_n = n // (PLANE * CORES)
+    slab = ints_raw.shape[1]
+    width = slab // COLUMN_BLOCKS
+    blocks = send.shape[1] // (n * pair_dev)
+    per_copy = pair_dev * blocks
+    chunk_d = blocks * LANES
+    core = lax.rem(me, CORES)
+    plane = lax.rem(me // CORES, PLANE)
+    depth = me // (CORES * PLANE)
+
+    barrier = pltpu.get_barrier_semaphore()
+
+    @pl.loop(1, n)
+    def _(step):
+        pl.semaphore_signal(barrier, inc=1, **to(lax.rem(me + step, n)))
+
+    load_singles = pltpu.make_async_copy(singles_hbm, singles_ref, local_sem.at[0])
+    load_singles.start()
+    piece = nv // ints_sem.shape[0]
+    load_ints = []
+    for b in range(ints_sem.shape[0]):
+        rows = pl.ds(b * piece, piece)
+        load_ints.append(
+            pltpu.make_async_copy(ints_hbm.at[rows], ints_raw.at[rows], ints_sem.at[b])
+        )
+        load_ints[-1].start()
+
+    def fill(chunk):
+        for j in range(blocks):
+            first = (chunk * blocks + j) * LANES
+            have = min(LANES, nv - first)
+            for p in range(pair_dev):
+                if have > 0:
+                    value = amp_ref[p, 0, :, first : first + have]
+                    if have < LANES:
+                        value = jnp.concatenate(
+                            [value, jnp.zeros((nc, LANES - have), F32)], axis=1
+                        )
+                else:
+                    value = jnp.zeros((nc, LANES), F32)
+                send[chunk, pl.ds(p * blocks + j, nc, stride=per_copy), :] = value
+
+    def block_copy(chunk, target):
+        source = pl.ds(pl.multiple_of(target * per_copy, 8), per_copy)
+        landing = pl.ds(pl.multiple_of(me * per_copy, 8), per_copy)
+        return pltpu.make_async_remote_copy(
+            src_ref=send.at[chunk, source],
+            dst_ref=recv.at[chunk, landing],
+            send_sem=a2a_send.at[chunk],
+            recv_sem=a2a_recv.at[chunk],
+            **to(target),
+        )
+
+    def start_chunk(chunk):
+        @pl.loop(1, n)
+        def _(step):
+            block_copy(chunk, lax.rem(me + step, n)).start()
+
+        mine = pl.ds(pl.multiple_of(me * per_copy, 8), per_copy)
+        pltpu.make_async_copy(
+            send.at[chunk, mine], recv.at[chunk, mine], a2a_recv.at[chunk]
+        ).start()
+
+    fill(0)
+    pl.semaphore_wait(barrier, n - 1)
+    start_chunk(0)
+    for chunk in range(1, CHUNKS):
+        fill(chunk)
+        start_chunk(chunk)
+
+    table_rows = vir_ref.shape[0]
+
+    def vir_of(which):
+        orbital = slab_ref[pl.ds(which, 1), :]
+        lane = jnp.bitwise_and(orbital, LANES - 1)
+        row = jnp.right_shift(orbital, 7)
+        hot = (lax.broadcasted_iota(jnp.int32, (LANES, slab), 0) == lane).astype(F32)
+        table = jnp.dot(
+            vir_ref[...], hot, precision=lax.Precision.HIGHEST, preferred_element_type=F32
+        )
+        at_row = lax.broadcasted_iota(jnp.int32, (table_rows, slab), 0) == row
+        return jnp.sum(jnp.where(at_row, table, 0.0), axis=0, keepdims=True)
+
+    no = occ_ref.shape[1]
+    own_iota = lax.broadcasted_iota(jnp.int32, (pair_dev, no), 1)
+
+    def occ_of(which):
+        hot = own_iota == own_ref[:, which : which + 1]
+        return jnp.sum(jnp.where(hot, occ_ref[...], 0.0), axis=1, keepdims=True)
+
+    denom_ref[...] = vir_of(0) + vir_of(1) - occ_of(0) - occ_of(1)
+
+    load_singles.wait()
+    column = singles_ref[pl.ds(me, 1), :]
+    pair_iota = lax.broadcasted_iota(jnp.int32, (pairs, no), 1)
+    hot_i = pair_iota == pair_ref[:, 0:1]
+    hot_j = pair_iota == pair_ref[:, 1:2]
+    first_window = jnp.sum(jnp.where(hot_i, column, 0.0), axis=1, keepdims=True)
+    second_window = jnp.sum(jnp.where(hot_j, column, 0.0), axis=1, keepdims=True)
+    weights = jnp.where(hot_j, first_window, 0.0) - jnp.where(hot_i, second_window, 0.0)
+    for chunk in range(CHUNKS):
+        first = chunk * chunk_d
+        have = min(chunk_d, nv - first)
+        value = lax.dot_general(
+            weights,
+            singles_ref[first : first + have, :],
+            (((1,), (1,)), ((), ())),
+            precision=lax.Precision.HIGHEST,
+            preferred_element_type=F32,
+        )
+        if have < chunk_d:
+            value = jnp.concatenate([value, jnp.zeros((pairs, chunk_d - have), F32)], axis=1)
+        spart[chunk] = value
+
+    for b in range(len(load_ints)):
+        load_ints[b].wait()
+
+        @pl.loop(0, piece // 16)
+        def _(i):
+            at = pl.ds(pl.multiple_of(b * piece + i * 16, 16), 16)
+            high, low = split_two(ints_raw[at, :])
+            ints_high[at, :] = high
+            ints_low[at, :] = low
+
+    padded = CHUNKS * chunk_d
+    if padded > nv:
+        ints_high[nv:padded, :] = jnp.zeros((padded - nv, slab), BF16)
+        ints_low[nv:padded, :] = jnp.zeros((padded - nv, slab), BF16)
+
+    pair_row = lax.broadcasted_iota(jnp.int32, (pairs, pairs), 0)
+    slot = lax.rem(pair_row, pair_dev)
+    rest = pair_row // pair_dev
+    at_depth = lax.rem(rest, depth_n)
+    rest = rest // depth_n
+    pair_of_row = (at_depth * PLANE * CORES + lax.rem(rest, PLANE) * CORES + rest // PLANE) * pair_dev + slot
+    pair_column = lax.broadcasted_iota(jnp.int32, (pairs, pairs), 1)
+    unpack = (
+        (pair_column == pair_of_row).astype(F32) - (pair_column == mirror_ref[...]).astype(F32)
+    ).astype(BF16)
+
+    half = pairs // CORES
+    plane_rows = half // PLANE
+
+    def tau_parts(chunk):
+        whole = recv.at[chunk]
+        pltpu.make_async_copy(whole, whole, a2a_recv.at[chunk]).wait()
+        for j in range(blocks):
+            rows_ref[:, j * LANES : (j + 1) * LANES] = recv[chunk, pl.ds(j, pairs, stride=blocks), :]
+        value = rows_ref[...]
+        one, two = split_two(value)
+        three = (value - one.astype(F32) - two.astype(F32)).astype(BF16)
+        tau = (bf16_dot(unpack, one) + bf16_dot(unpack, two)) + bf16_dot(unpack, three)
+        return split_two(tau + spart[chunk])
+
+    def product(chunk, parts, nb):
+        high, low = parts
+        at = pl.ds(chunk * chunk_d, chunk_d)
+        columns = pl.ds(nb * width, width)
+        right = ints_high[at, columns]
+        value = bf16_dot(high, right) + bf16_dot(low, right)
+        value = value + bf16_dot(high, ints_low[at, columns])
+        return value.reshape(CORES, PLANE, plane_rows, width)
+
+    for chunk in range(CHUNKS - 1):
+        parts = tau_parts(chunk)
+        for nb in range(COLUMN_BLOCKS):
+            value = product(chunk, parts, nb)
+            partial[nb] = value if chunk == 0 else partial[nb] + value
+    parts = tau_parts(CHUNKS - 1)
+
+    def core_copy(nb):
+        return pltpu.make_async_remote_copy(
+            src_ref=partial.at[nb, 1 - core],
+            dst_ref=got_core.at[nb],
+            send_sem=core_send.at[nb],
+            recv_sem=core_recv.at[nb],
+            **to(me + 1 - 2 * core),
+        )
+
+    def plane_copy(nb, step):
+        other = lax.rem(plane + step, PLANE)
+        return pltpu.make_async_remote_copy(
+            src_ref=partial.at[nb, core, other],
+            dst_ref=got_plane.at[nb, step - 1],
+            send_sem=plane_send.at[nb, step - 1],
+            recv_sem=plane_recv.at[nb, step - 1],
+            **to((depth * PLANE + other) * CORES + core),
+        )
+
+    def depth_copy(nb, step):
+        other = lax.rem(depth + step, depth_n)
+        return pltpu.make_async_remote_copy(
+            src_ref=ready_depth.at[nb, other],
+            dst_ref=got_depth.at[nb, step - 1],
+            send_sem=depth_send.at[nb, step - 1],
+            recv_sem=depth_recv.at[nb, step - 1],
+            **to((other * PLANE + plane) * CORES + core),
+        )
+
+    def contract(nb):
+        value = product(CHUNKS - 1, parts, nb)
+        partial[nb] = partial[nb] + value if CHUNKS > 1 else value
+        core_copy(nb).start()
+
+    def add_core(nb):
+        core_copy(nb).wait_recv()
+        partial[nb, core] = partial[nb, core] + got_core[nb]
+        for step in range(1, PLANE):
+            plane_copy(nb, step).start()
+
+    def add_plane(nb):
+        for step in range(1, PLANE):
+            plane_copy(nb, step).wait_recv()
+        value = partial[nb, core, plane]
+        for step in range(1, PLANE):
+            value = value + got_plane[nb, step - 1]
+        for z in range(depth_n):
+            ready_depth[nb, z] = value[z * pair_dev : (z + 1) * pair_dev]
+        for step in range(1, depth_n):
+            depth_copy(nb, step).start()
+
+    def add_depth(nb):
+        for step in range(1, depth_n):
+            depth_copy(nb, step).wait_recv()
+        value = ready_depth[nb, depth]
+        for step in range(1, depth_n):
+            value = value + got_depth[nb, step - 1]
+        columns = slice(nb * width, (nb + 1) * width)
+        out_ref[:, columns] = 0.5 * value / denom_ref[:, columns]
+
+    for step in range(COLUMN_BLOCKS + 3):
+        for lag, stage in enumerate((contract, add_core, add_plane, add_depth)):
+            if 0 <= step - lag < COLUMN_BLOCKS:
+                stage(step - lag)
+
+    for nb in range(COLUMN_BLOCKS):
+        core_copy(nb).wait_send()
+        for step in range(1, PLANE):
+            plane_copy(nb, step).wait_send()
+        for step in range(1, depth_n):
+            depth_copy(nb, step).wait_send()
+    for chunk in range(CHUNKS):
+        @pl.loop(1, n)
+        def _(step):
+            block_copy(chunk, lax.rem(me + step, n)).wait_send()
+
+
+def kernel_body(n, amplitudes, singles, pair_list, mirror, slab_rows, occ_energy, vir_energy, integrals):
+    pair_dev, _, nc, nv = amplitudes.shape
+    slab = integrals.shape[0]
+    no = singles.shape[0]
+    pairs = pair_dev * n
+    depth_n = n // (PLANE * CORES)
+    member = lax.axis_index("mem")
+    blocks = -(-nv // (LANES * CHUNKS))
+    padded = blocks * CHUNKS * LANES
+    width = slab // COLUMN_BLOCKS
+
+    def in_row_order(values):
+        cut = values.reshape(depth_n, PLANE, CORES, pair_dev, -1)
+        return cut.transpose(2, 1, 0, 3, 4).reshape(pairs, -1)
+
+    own = lax.dynamic_slice_in_dim(pair_list, member * pair_dev, pair_dev, 0)
+    table = jnp.pad(vir_energy, (0, -nv % LANES)).reshape(-1, LANES)
+    ints = jnp.transpose(integrals, (1, 2, 3, 0)).reshape(nv, slab)
+    pieces = max(k for k in range(1, 9) if nv % (16 * k) == 0)
+    vmem = pl.BlockSpec(memory_space=pltpu.VMEM)
+    hbm = pl.BlockSpec(memory_space=pl.ANY)
+    dma = pltpu.SemaphoreType.DMA
+    plane_rows = pairs // (CORES * PLANE)
+    return pl.pallas_call(
+        functools.partial(ladder_kernel, n),
+        out_shape=jax.ShapeDtypeStruct((pair_dev, slab), F32),
+        in_specs=[vmem] * 7 + [hbm] * 2,
+        out_specs=vmem,
+        scratch_shapes=[
+            pltpu.VMEM((CHUNKS, pairs * blocks, LANES), F32),
+            pltpu.VMEM((CHUNKS, pairs * blocks, LANES), F32),
+            pltpu.VMEM((nv, no), F32),
+            pltpu.VMEM((nv, slab), F32),
+            pltpu.VMEM((padded, slab), BF16),
+            pltpu.VMEM((padded, slab), BF16),
+            pltpu.VMEM((CHUNKS, pairs, blocks * LANES), F32),
+            pltpu.VMEM((pairs, blocks * LANES), F32),
+            pltpu.VMEM((COLUMN_BLOCKS, CORES, PLANE, plane_rows, width), F32),
+            pltpu.VMEM((COLUMN_BLOCKS, PLANE, plane_rows, width), F32),
+            pltpu.VMEM((COLUMN_BLOCKS, PLANE - 1, plane_rows, width), F32),
+            pltpu.VMEM((COLUMN_BLOCKS, depth_n, pair_dev, width), F32),
+            pltpu.VMEM((COLUMN_BLOCKS, depth_n - 1, pair_dev, width), F32),
+            pltpu.VMEM((pair_dev, slab), F32),
+            dma((1,)),
+            dma((pieces,)),
+            dma((CHUNKS,)),
+            dma((CHUNKS,)),
+            dma((COLUMN_BLOCKS,)),
+            dma((COLUMN_BLOCKS,)),
+            dma((COLUMN_BLOCKS, PLANE - 1)),
+            dma((COLUMN_BLOCKS, PLANE - 1)),
+            dma((COLUMN_BLOCKS, depth_n - 1)),
+            dma((COLUMN_BLOCKS, depth_n - 1)),
+        ],
+        compiler_params=pltpu.CompilerParams(
+            collective_id=0, has_side_effects=True, vmem_limit_bytes=58 * 2**20
+        ),
+    )(
+        amplitudes,
+        in_row_order(mirror),
+        in_row_order(pair_list),
+        own,
+        slab_rows.T,
+        occ_energy[None, :],
+        table,
+        singles.T,
+        ints,
+    )
+
+
+def grouped_body(amplitudes, singles, pair_list, mirror, slab_rows, occ_energy, vir_energy, integrals):
     owners = lax.axis_size("mem")
     member = lax.axis_index("mem")
     pair_dev = amplitudes.shape[0]
@@ -58,6 +440,10 @@
 
 
 def solution(mesh):
+    owners = mesh.shape["mem"]
+    body = grouped_body
+    if mesh.shape["grp"] == 1 and owners % (2 * PLANE * CORES) == 0:
+        body = functools.partial(kernel_body, owners)
     in_specs = (
         P("mem", "grp", None, None),
         P(),

time: 192 us -> 73 us (0.38)
  blocking collectives: 80.8 us -> 0 us
  Pallas kernels: 0 us -> 65.2 us
  local copies, waits for them, and re-layouts: 46.6 us -> 7.4 us
  starting transfers between devices: 26.3 us -> 0 us
  matrix products: 17.4 us -> 0 us
  waiting for transfers between devices: 15.4 us -> 0 us
  other arithmetic: 3.97 us -> 0 us
    unnamed x1 -> x0, blocking collectives: 80.8 us -> none
    pallas_call x0 -> x1, Pallas kernels: none -> 65.2 us  [kernel_body(): pl.pallas_call(functools.partial(ladder_kernel, n), out_shape=jax.ShapeDt...]
    gather x7 -> x0, local copies, waits for them, and re-layouts: 31.9 us -> none  [the longest x1 11.8 us: body(): vir_second = jnp.take(vir_energy, slab_rows[:, 1])]
    unnamed x8 -> x0, starting transfers between devices: 18.8 us -> none
    dot_general x1 -> x0, matrix products: 17.4 us -> none  [body(): lax.dot_general(flat_tau, flat_ints, (((1,), (1,)), ((), ())), precision=...]
    all_to_all x1 -> x0, waiting for transfers between devices: 13.6 us -> none  [body(): lax.all_to_all(quarters, 'mem', split_axis=2, concat_axis=0, tiled=True)]
    all_to_all x1 -> x0, starting transfers between devices: 7.43 us -> none  [body(): lax.all_to_all(quarters, 'mem', split_axis=2, concat_axis=0, tiled=True)]
    all_to_all x3 -> x0, local copies, waits for them, and re-layouts: 6.42 us -> none  [body(): lax.all_to_all(quarters, 'mem', split_axis=2, concat_axis=0, tiled=True)]
  transfers between devices with their start and end apart: 9 -> 0, of which waited for: 2 -> 0; matrix products, arithmetic and copies ran while one was open for 18% -> 0% of each run, Pallas kernels for 0% -> 0%
where the time goes in v1:
time: 73 us; the launch traced here: 72.7 us
  Pallas kernels  65.2 us (89%)
  local copies, waits for them, and re-layouts  7.4 us (10%)
    pallas_call x1, Pallas kernels, kernel_body(): pl.pallas_call(functools.partial(ladder_kernel, n), out_shape=jax.ShapeDt...  65.2 us
    unnamed x2, local copies, waits for them, and re-layouts  2.15 us
    reshape x3, local copies, waits for them, and re-layouts, in_row_order(): cut = values.reshape(depth_n, PLANE, CORES, pair_dev, -1)  1.6 us
    reshape x3, local copies, waits for them, and re-layouts, in_row_order(): return cut.transpose(2, 1, 0, 3, 4).reshape(pairs, -1)  1.59 us

profile of v1, /device:TPU:0, one launch (start us, length us, event | category | flops | bytes accessed | tf_op | source)
XLA Modules:
  0.0 72.7 jit_solution(14024606640647996673)
XLA Ops:
  0.0 0.8 %constant_dynamic-slice_fusion = s32[6,2]{0,1:T(2,128)S(1)} fusion(s32[192,2]{0,1:T(2,128)} %param.10, s32[]{:T(128)S(6)} %select_n.3), kind=kLoop, calls=%fused_computation.2 | loop fusion | bytes 100 | tf_op jit(solution)/shard_map/dynamic_slice | solution.py:334
  0.8 0.7 copy.16.own_ref
  1.4 1.3 %pad_bitcast_fusion.vir_ref = f32[16,128]{1,0:T(8,128)} fusion(f32[2000]{0:T(1024)} %param.14), kind=kLoop, calls=%fused_computation.1 | loop fusion | bytes 16192 | tf_op jit(solution)/shard_map/reshape | solution.py:335
  2.7 0.8 %reshape.18 = s32[4,4,2,6,1]{3,2,1,0,4:T(2,128)S(1)} reshape(s32[192]{0:T(256)} %param.11) | data formatting | bytes 1536 | tf_op jit(solution)/shard_map/reshape | solution.py:331
  3.5 0.8 %reshape.20 = s32[4,4,2,6,2]{3,2,1,0,4:T(2,128)S(1)} reshape(s32[192,2]{0,1:T(2,128)} %param.10) | data formatting | bytes 3072 | tf_op jit(solution)/shard_map/reshape | solution.py:331
  4.4 0.1 reshape.21
  4.5 0.7 reshape.24.mirror_ref
  5.2 0.8 %copy.15.pair_ref = s32[192,2]{1,0:T(8,128)} copy(s32[192,2]{0,1:T(2,128)S(1)} %reshape.21) | data formatting | bytes 3072 | tf_op jit(solution)/shard_map/reshape | solution.py:332
  6.0 65.2 %shard_map.82 = f32[6,2048]{1,0:T(8,128)} custom-call(f32[6,1,32,2000]{3,2,1,0:T(8,128)} %amp_ref.1, s32[192,1]{1,0:T(8,128)} %reshape.24.mirror_ref, s32[192,2]{1,0:T(8,128)} %copy.15.pair_ref, s32[6,2]{1,0:T(8,128)} %copy.16.own_ref, s32[2,2048]{1,0:T(2,128)} %bitcast.22, f32[1,250]{1,0:T(1,128)} %bitcast.23, f32[16,128]{1,0:T(8,128)} %pad_bitcast_fusion.vir_ref, ...), custom_call_target="tpu_custom_call" | custom-call | tf_op jit(solution)/shard_map/pallas_call | solution.py:342
  71.2 1.5 %copy.20 = f32[6,2048]{1,0:T(8,128)} copy(f32[6,2048]{1,0:T(8,128)} %shard_map.82) | data formatting | bytes 98304
  (2 shorter events, 0.0 us)

commit v2 on v1

--- a/solution.py
+++ b/solution.py
@@ -34,7 +34,6 @@
     amp_ref,
     mirror_ref,
     pair_ref,
-    own_ref,
     slab_ref,
     occ_ref,
     vir_ref,
@@ -55,6 +54,7 @@
     ready_depth,
     got_depth,
     denom_ref,
+    table_ref,
     local_sem,
     ints_sem,
     a2a_send,
@@ -139,7 +139,12 @@
         fill(chunk)
         start_chunk(chunk)
 
-    table_rows = vir_ref.shape[0]
+    table_rows = table_ref.shape[0]
+    table_ref[...] = jnp.zeros_like(table_ref)
+    energies = vir_ref[...].reshape(1, nv)
+    for r in range(table_rows):
+        have = min(LANES, nv - r * LANES)
+        table_ref[r : r + 1, :have] = energies[:, r * LANES : r * LANES + have]
 
     def vir_of(which):
         orbital = slab_ref[pl.ds(which, 1), :]
@@ -147,27 +152,48 @@
         row = jnp.right_shift(orbital, 7)
         hot = (lax.broadcasted_iota(jnp.int32, (LANES, slab), 0) == lane).astype(F32)
         table = jnp.dot(
-            vir_ref[...], hot, precision=lax.Precision.HIGHEST, preferred_element_type=F32
+            table_ref[...], hot, precision=lax.Precision.HIGHEST, preferred_element_type=F32
         )
         at_row = lax.broadcasted_iota(jnp.int32, (table_rows, slab), 0) == row
         return jnp.sum(jnp.where(at_row, table, 0.0), axis=0, keepdims=True)
 
-    no = occ_ref.shape[1]
-    own_iota = lax.broadcasted_iota(jnp.int32, (pair_dev, no), 1)
+    no = occ_ref.shape[0]
+    occ = occ_ref[...].reshape(1, no)
+    orbitals = pair_ref[...].astype(F32)
+    own_hot = lax.broadcasted_iota(jnp.int32, (pair_dev, pairs), 1) == (
+        lax.broadcasted_iota(jnp.int32, (pair_dev, pairs), 0) + me * pair_dev
+    )
+    own_iota = lax.broadcasted_iota(jnp.int32, (pair_dev, no), 1).astype(F32)
+
+    def pick(hot, row):
+        return jnp.sum(jnp.where(hot, row, 0.0), axis=1, keepdims=True)
+
 
     def occ_of(which):
-        hot = own_iota == own_ref[:, which : which + 1]
-        return jnp.sum(jnp.where(hot, occ_ref[...], 0.0), axis=1, keepdims=True)
+        return pick(own_iota == pick(own_hot, orbitals[which : which + 1]), occ)
 
     denom_ref[...] = vir_of(0) + vir_of(1) - occ_of(0) - occ_of(1)
+
+    pair_row = lax.broadcasted_iota(jnp.int32, (pairs, pairs), 0)
+    slot = lax.rem(pair_row, pair_dev)
+    rest = pair_row // pair_dev
+    at_depth = lax.rem(rest, depth_n)
+    rest = rest // depth_n
+    pair_of_row = (at_depth * PLANE * CORES + lax.rem(rest, PLANE) * CORES + rest // PLANE) * pair_dev + slot
+    pair_column = lax.broadcasted_iota(jnp.int32, (pairs, pairs), 1)
+    in_order = pair_column == pair_of_row
+    partner = pick(in_order, mirror_ref[...].reshape(1, pairs).astype(F32))
+    unpack = (
+        in_order.astype(F32) - (pair_column.astype(F32) == partner).astype(F32)
+    ).astype(BF16)
 
     load_singles.wait()
     column = singles_ref[pl.ds(me, 1), :]
-    pair_iota = lax.broadcasted_iota(jnp.int32, (pairs, no), 1)
-    hot_i = pair_iota == pair_ref[:, 0:1]
-    hot_j = pair_iota == pair_ref[:, 1:2]
-    first_window = jnp.sum(jnp.where(hot_i, column, 0.0), axis=1, keepdims=True)
-    second_window = jnp.sum(jnp.where(hot_j, column, 0.0), axis=1, keepdims=True)
+    pair_iota = lax.broadcasted_iota(jnp.int32, (pairs, no), 1).astype(F32)
+    hot_i = pair_iota == pick(in_order, orbitals[0:1])
+    hot_j = pair_iota == pick(in_order, orbitals[1:2])
+    first_window = pick(hot_i, column)
+    second_window = pick(hot_j, column)
     weights = jnp.where(hot_j, first_window, 0.0) - jnp.where(hot_i, second_window, 0.0)
     for chunk in range(CHUNKS):
         first = chunk * chunk_d
@@ -198,17 +224,6 @@
         ints_high[nv:padded, :] = jnp.zeros((padded - nv, slab), BF16)
         ints_low[nv:padded, :] = jnp.zeros((padded - nv, slab), BF16)
 
-    pair_row = lax.broadcasted_iota(jnp.int32, (pairs, pairs), 0)
-    slot = lax.rem(pair_row, pair_dev)
-    rest = pair_row // pair_dev
-    at_depth = lax.rem(rest, depth_n)
-    rest = rest // depth_n
-    pair_of_row = (at_depth * PLANE * CORES + lax.rem(rest, PLANE) * CORES + rest // PLANE) * pair_dev + slot
-    pair_column = lax.broadcasted_iota(jnp.int32, (pairs, pairs), 1)
-    unpack = (
-        (pair_column == pair_of_row).astype(F32) - (pair_column == mirror_ref[...]).astype(F32)
-    ).astype(BF16)
-
     half = pairs // CORES
     plane_rows = half // PLANE
 
@@ -297,7 +312,7 @@
         for step in range(1, depth_n):
             value = value + got_depth[nb, step - 1]
         columns = slice(nb * width, (nb + 1) * width)
-        out_ref[:, columns] = 0.5 * value / denom_ref[:, columns]
+        out_ref[:, columns] = value / denom_ref[:, columns]
 
     for step in range(COLUMN_BLOCKS + 3):
         for lag, stage in enumerate((contract, add_core, add_plane, add_depth)):
@@ -322,27 +337,20 @@
     no = singles.shape[0]
     pairs = pair_dev * n
     depth_n = n // (PLANE * CORES)
-    member = lax.axis_index("mem")
     blocks = -(-nv // (LANES * CHUNKS))
     padded = blocks * CHUNKS * LANES
     width = slab // COLUMN_BLOCKS
 
-    def in_row_order(values):
-        cut = values.reshape(depth_n, PLANE, CORES, pair_dev, -1)
-        return cut.transpose(2, 1, 0, 3, 4).reshape(pairs, -1)
-
-    own = lax.dynamic_slice_in_dim(pair_list, member * pair_dev, pair_dev, 0)
-    table = jnp.pad(vir_energy, (0, -nv % LANES)).reshape(-1, LANES)
     ints = jnp.transpose(integrals, (1, 2, 3, 0)).reshape(nv, slab)
     pieces = max(k for k in range(1, 9) if nv % (16 * k) == 0)
     vmem = pl.BlockSpec(memory_space=pltpu.VMEM)
     hbm = pl.BlockSpec(memory_space=pl.ANY)
     dma = pltpu.SemaphoreType.DMA
     plane_rows = pairs // (CORES * PLANE)
-    return pl.pallas_call(
+    scaled = pl.pallas_call(
         functools.partial(ladder_kernel, n),
         out_shape=jax.ShapeDtypeStruct((pair_dev, slab), F32),
-        in_specs=[vmem] * 7 + [hbm] * 2,
+        in_specs=[vmem] * 6 + [hbm] * 2,
         out_specs=vmem,
         scratch_shapes=[
             pltpu.VMEM((CHUNKS, pairs * blocks, LANES), F32),
@@ -359,6 +367,7 @@
             pltpu.VMEM((COLUMN_BLOCKS, depth_n, pair_dev, width), F32),
             pltpu.VMEM((COLUMN_BLOCKS, depth_n - 1, pair_dev, width), F32),
             pltpu.VMEM((pair_dev, slab), F32),
+            pltpu.VMEM((-(-nv // LANES), LANES), F32),
             dma((1,)),
             dma((pieces,)),
             dma((CHUNKS,)),
@@ -375,15 +384,15 @@
         ),
     )(
         amplitudes,
-        in_row_order(mirror),
-        in_row_order(pair_list),
-        own,
+        mirror,
+        pair_list.T,
         slab_rows.T,
-        occ_energy[None, :],
-        table,
+        occ_energy,
+        vir_energy,
         singles.T,
         ints,
     )
+    return 0.5 * scaled
 
 
 def grouped_body(amplitudes, singles, pair_list, mirror, slab_rows, occ_energy, vir_energy, integrals):

time: 73 us -> 66.9 us (0.916)
  local copies, waits for them, and re-layouts: 7.4 us -> 0 us
  other arithmetic: 0 us -> 1.48 us
    reshape x7 -> x0, local copies, waits for them, and re-layouts: 4.49 us -> none  [the longest x3 1.6 us: in_row_order(): cut = values.reshape(depth_n, PLANE, CORES, pair_dev, -1)]
    unnamed x2 -> x0, local copies, waits for them, and re-layouts: 2.15 us -> none
    mul x0 -> x1, other arithmetic: none -> 1.48 us  [kernel_body(): return 0.5 * scaled]
    dynamic_slice x1 -> x0, local copies, waits for them, and re-layouts: 0.75 us -> none  [kernel_body(): own = lax.dynamic_slice_in_dim(pair_list, member * pair_dev, pair_dev, 0)]
where the time goes in v2:
time: 66.9 us; the launch traced here: 66.7 us
  Pallas kernels  65.2 us (97%)
  other arithmetic  1.48 us (2%)
    pallas_call x1, Pallas kernels, kernel_body(): pl.pallas_call(functools.partial(ladder_kernel, n), out_shape=jax.ShapeDt...  65.2 us
    mul x1, other arithmetic, kernel_body(): return 0.5 * scaled  1.48 us

profile of v2, /device:TPU:0, one launch (start us, length us, event | category | flops | bytes accessed | tf_op | source)
XLA Modules:
  0.0 66.7 jit_solution(11389743809866235645)
XLA Ops:
  0.0 65.2 %shard_map.82 = f32[6,2048]{1,0:T(8,128)} custom-call(f32[6,1,32,2000]{3,2,1,0:T(8,128)} %amp_ref.1, s32[192]{0:T(256)} %mirror_ref.1, s32[2,192]{1,0:T(2,128)} %bitcast.9, s32[2,2048]{1,0:T(2,128)} %bitcast.8, f32[250]{0:T(256)} %occ_ref.1, f32[2000]{0:T(1024)} %vir_ref.1, f32[2000,250]{1,0:T(8,128)} %bitcast.7, f32[2000,2048]{1,0:T(8,128)} %bitcast.6), custom_call_target="tpu_custom_call" | custom-call | tf_op jit(solution)/shard_map/pallas_call | solution.py:350
  65.2 1.5 %broadcast_multiply_fusion = f32[6,2048]{1,0:T(8,128)} fusion(f32[6,2048]{1,0:T(8,128)} %shard_map.82), kind=kLoop, calls=%fused_computation | loop fusion | flops 12288 | bytes 98304 | tf_op jit(solution)/shard_map/mul | solution.py:395

commit v3 on v2

--- a/solution.py
+++ b/solution.py
@@ -10,7 +10,6 @@
 F32 = jnp.float32
 BF16 = jnp.bfloat16
 LANES = 128
-CHUNKS = 2
 COLUMN_BLOCKS = 4
 PLANE = 4
 CORES = 2
@@ -72,9 +71,11 @@
     depth_n = n // (PLANE * CORES)
     slab = ints_raw.shape[1]
     width = slab // COLUMN_BLOCKS
-    blocks = send.shape[1] // (n * pair_dev)
+    blocks = -(-nv // LANES)
     per_copy = pair_dev * blocks
-    chunk_d = blocks * LANES
+    padded = blocks * LANES
+    half = pairs // CORES
+    plane_rows = half // PLANE
     core = lax.rem(me, CORES)
     plane = lax.rem(me // CORES, PLANE)
     depth = me // (CORES * PLANE)
@@ -96,48 +97,42 @@
         )
         load_ints[-1].start()
 
-    def fill(chunk):
-        for j in range(blocks):
-            first = (chunk * blocks + j) * LANES
-            have = min(LANES, nv - first)
-            for p in range(pair_dev):
-                if have > 0:
-                    value = amp_ref[p, 0, :, first : first + have]
-                    if have < LANES:
-                        value = jnp.concatenate(
-                            [value, jnp.zeros((nc, LANES - have), F32)], axis=1
-                        )
-                else:
-                    value = jnp.zeros((nc, LANES), F32)
-                send[chunk, pl.ds(p * blocks + j, nc, stride=per_copy), :] = value
-
-    def block_copy(chunk, target):
+    for j in range(blocks):
+        first = j * LANES
+        have = min(LANES, nv - first)
+        for p in range(pair_dev):
+            value = amp_ref[p, 0, :, first : first + have]
+            if have < LANES:
+                value = jnp.concatenate([value, jnp.zeros((nc, LANES - have), F32)], axis=1)
+            send[pl.ds(p * blocks + j, nc, stride=per_copy), :] = value
+
+    landing = pl.ds(pl.multiple_of((me // CORES) * per_copy, 8), per_copy)
+
+    def block_copy(target):
         source = pl.ds(pl.multiple_of(target * per_copy, 8), per_copy)
-        landing = pl.ds(pl.multiple_of(me * per_copy, 8), per_copy)
         return pltpu.make_async_remote_copy(
-            src_ref=send.at[chunk, source],
-            dst_ref=recv.at[chunk, landing],
-            send_sem=a2a_send.at[chunk],
-            recv_sem=a2a_recv.at[chunk],
+            src_ref=send.at[source],
+            dst_ref=recv.at[core, landing],
+            send_sem=a2a_send.at[0],
+            recv_sem=a2a_recv.at[core],
             **to(target),
         )
 
-    def start_chunk(chunk):
+    def start_blocks():
         @pl.loop(1, n)
         def _(step):
-            block_copy(chunk, lax.rem(me + step, n)).start()
+            block_copy(lax.rem(me + step, n)).start()
 
         mine = pl.ds(pl.multiple_of(me * per_copy, 8), per_copy)
         pltpu.make_async_copy(
-            send.at[chunk, mine], recv.at[chunk, mine], a2a_recv.at[chunk]
+            send.at[mine], recv.at[core, landing], a2a_recv.at[core]
         ).start()
 
-    fill(0)
     pl.semaphore_wait(barrier, n - 1)
-    start_chunk(0)
-    for chunk in range(1, CHUNKS):
-        fill(chunk)
-        start_chunk(chunk)
+
+    @pl.when(core == 0)
+    def _():
+        start_blocks()
 
     table_rows = table_ref.shape[0]
     table_ref[...] = jnp.zeros_like(table_ref)
@@ -183,9 +178,16 @@
     pair_column = lax.broadcasted_iota(jnp.int32, (pairs, pairs), 1)
     in_order = pair_column == pair_of_row
     partner = pick(in_order, mirror_ref[...].reshape(1, pairs).astype(F32))
-    unpack = (
-        in_order.astype(F32) - (pair_column.astype(F32) == partner).astype(F32)
-    ).astype(BF16)
+    group_column = lax.broadcasted_iota(jnp.int32, (half, half), 1)
+
+    def unpack_of(group):
+        pair_here = (group_column // pair_dev * CORES + group) * pair_dev + lax.rem(
+            group_column, pair_dev
+        )
+        rows = slice(group * half, (group + 1) * half)
+        same = pair_here == pair_of_row[rows, :half]
+        mirrored = pair_here.astype(F32) == partner[rows]
+        return (same.astype(F32) - mirrored.astype(F32)).astype(BF16)
 
     load_singles.wait()
     column = singles_ref[pl.ds(me, 1), :]
@@ -195,19 +197,19 @@
     first_window = pick(hot_i, column)
     second_window = pick(hot_j, column)
     weights = jnp.where(hot_j, first_window, 0.0) - jnp.where(hot_i, second_window, 0.0)
-    for chunk in range(CHUNKS):
-        first = chunk * chunk_d
-        have = min(chunk_d, nv - first)
-        value = lax.dot_general(
-            weights,
-            singles_ref[first : first + have, :],
-            (((1,), (1,)), ((), ())),
-            precision=lax.Precision.HIGHEST,
-            preferred_element_type=F32,
-        )
-        if have < chunk_d:
-            value = jnp.concatenate([value, jnp.zeros((pairs, chunk_d - have), F32)], axis=1)
-        spart[chunk] = value
+    singles_part = lax.dot_general(
+        weights,
+        singles_ref[...],
+        (((1,), (1,)), ((), ())),
+        precision=lax.Precision.HIGHEST,
+        preferred_element_type=F32,
+    )
+    if padded > nv:
+        singles_part = jnp.concatenate(
+            [singles_part, jnp.zeros((pairs, padded - nv), F32)], axis=1
+        )
+    for group in range(CORES):
+        spart[group] = singles_part[group * half : (group + 1) * half]
 
     for b in range(len(load_ints)):
         load_ints[b].wait()
@@ -219,54 +221,37 @@
             ints_high[at, :] = high
             ints_low[at, :] = low
 
-    padded = CHUNKS * chunk_d
     if padded > nv:
         ints_high[nv:padded, :] = jnp.zeros((padded - nv, slab), BF16)
         ints_low[nv:padded, :] = jnp.zeros((padded - nv, slab), BF16)
 
-    half = pairs // CORES
-    plane_rows = half // PLANE
-
-    def tau_parts(chunk):
-        whole = recv.at[chunk]
-        pltpu.make_async_copy(whole, whole, a2a_recv.at[chunk]).wait()
+    def wait_group(group):
+        whole = recv.at[group]
+        pltpu.make_async_copy(whole, whole, a2a_recv.at[group]).wait()
+
+    def tau_parts(group):
         for j in range(blocks):
-            rows_ref[:, j * LANES : (j + 1) * LANES] = recv[chunk, pl.ds(j, pairs, stride=blocks), :]
+            rows_ref[:, j * LANES : (j + 1) * LANES] = recv[group, pl.ds(j, half, stride=blocks), :]
         value = rows_ref[...]
         one, two = split_two(value)
         three = (value - one.astype(F32) - two.astype(F32)).astype(BF16)
+        unpack = unpack_of(group)
         tau = (bf16_dot(unpack, one) + bf16_dot(unpack, two)) + bf16_dot(unpack, three)
-        return split_two(tau + spart[chunk])
-
-    def product(chunk, parts, nb):
-        high, low = parts
-        at = pl.ds(chunk * chunk_d, chunk_d)
-        columns = pl.ds(nb * width, width)
-        right = ints_high[at, columns]
-        value = bf16_dot(high, right) + bf16_dot(low, right)
-        value = value + bf16_dot(high, ints_low[at, columns])
-        return value.reshape(CORES, PLANE, plane_rows, width)
-
-    for chunk in range(CHUNKS - 1):
-        parts = tau_parts(chunk)
-        for nb in range(COLUMN_BLOCKS):
-            value = product(chunk, parts, nb)
-            partial[nb] = value if chunk == 0 else partial[nb] + value
-    parts = tau_parts(CHUNKS - 1)
-
-    def core_copy(nb):
+        return split_two(tau + spart[group])
+
+    def core_copy(group, nb):
         return pltpu.make_async_remote_copy(
-            src_ref=partial.at[nb, 1 - core],
+            src_ref=partial.at[group, nb],
             dst_ref=got_core.at[nb],
             send_sem=core_send.at[nb],
             recv_sem=core_recv.at[nb],
             **to(me + 1 - 2 * core),
         )
 
-    def plane_copy(nb, step):
+    def plane_copy(group, nb, step):
         other = lax.rem(plane + step, PLANE)
         return pltpu.make_async_remote_copy(
-            src_ref=partial.at[nb, core, other],
+            src_ref=partial.at[group, nb, other],
             dst_ref=got_plane.at[nb, step - 1],
             send_sem=plane_send.at[nb, step - 1],
             recv_sem=plane_recv.at[nb, step - 1],
@@ -283,21 +268,28 @@
             **to((other * PLANE + plane) * CORES + core),
         )
 
-    def contract(nb):
-        value = product(CHUNKS - 1, parts, nb)
-        partial[nb] = partial[nb] + value if CHUNKS > 1 else value
-        core_copy(nb).start()
-
-    def add_core(nb):
-        core_copy(nb).wait_recv()
-        partial[nb, core] = partial[nb, core] + got_core[nb]
+    def contract(group, parts, nb):
+        high, low = parts
+        columns = pl.ds(nb * width, width)
+        right = ints_high[:, columns]
+        value = bf16_dot(high, right) + bf16_dot(low, right)
+        value = value + bf16_dot(high, ints_low[:, columns])
+        partial[group, nb] = value.reshape(PLANE, plane_rows, width)
+
+        @pl.when(core != group)
+        def _():
+            core_copy(group, nb).start()
+
+    def add_core(group, nb):
+        core_copy(group, nb).wait_recv()
+        partial[group, nb] = partial[group, nb] + got_core[nb]
         for step in range(1, PLANE):
-            plane_copy(nb, step).start()
-
-    def add_plane(nb):
+            plane_copy(group, nb, step).start()
+
+    def add_plane(group, nb):
         for step in range(1, PLANE):
-            plane_copy(nb, step).wait_recv()
-        value = partial[nb, core, plane]
+            plane_copy(group, nb, step).wait_recv()
+        value = partial[group, nb, plane]
         for step in range(1, PLANE):
             value = value + got_plane[nb, step - 1]
         for z in range(depth_n):
@@ -305,7 +297,7 @@
         for step in range(1, depth_n):
             depth_copy(nb, step).start()
 
-    def add_depth(nb):
+    def add_depth(group, nb):
         for step in range(1, depth_n):
             depth_copy(nb, step).wait_recv()
         value = ready_depth[nb, depth]
@@ -314,21 +306,34 @@
         columns = slice(nb * width, (nb + 1) * width)
         out_ref[:, columns] = value / denom_ref[:, columns]
 
-    for step in range(COLUMN_BLOCKS + 3):
-        for lag, stage in enumerate((contract, add_core, add_plane, add_depth)):
-            if 0 <= step - lag < COLUMN_BLOCKS:
-                stage(step - lag)
+    for group in range(CORES):
+        wait_group(group)
+        if group == 0:
+            @pl.when(core == 1)
+            def _():
+                start_blocks()
+
+        parts = tau_parts(group)
+        for step in range(COLUMN_BLOCKS + 3):
+            if step < COLUMN_BLOCKS:
+                contract(group, parts, step)
+
+            @pl.when(core == group)
+            def _():
+                for lag, stage in enumerate((add_core, add_plane, add_depth)):
+                    if 0 <= step - lag - 1 < COLUMN_BLOCKS:
+                        stage(group, step - lag - 1)
 
     for nb in range(COLUMN_BLOCKS):
-        core_copy(nb).wait_send()
+        core_copy(0, nb).wait_send()
         for step in range(1, PLANE):
-            plane_copy(nb, step).wait_send()
+            plane_copy(0, nb, step).wait_send()
         for step in range(1, depth_n):
             depth_copy(nb, step).wait_send()
-    for chunk in range(CHUNKS):
-        @pl.loop(1, n)
-        def _(step):
-            block_copy(chunk, lax.rem(me + step, n)).wait_send()
+
+    @pl.loop(1, n)
+    def _(step):
+        block_copy(lax.rem(me + step, n)).wait_send()
 
 
 def kernel_body(n, amplitudes, singles, pair_list, mirror, slab_rows, occ_energy, vir_energy, integrals):
@@ -337,8 +342,9 @@
     no = singles.shape[0]
     pairs = pair_dev * n
     depth_n = n // (PLANE * CORES)
-    blocks = -(-nv // (LANES * CHUNKS))
-    padded = blocks * CHUNKS * LANES
+    blocks = -(-nv // LANES)
+    padded = blocks * LANES
+    half = pairs // CORES
     width = slab // COLUMN_BLOCKS
 
     ints = jnp.transpose(integrals, (1, 2, 3, 0)).reshape(nv, slab)
@@ -353,15 +359,15 @@
         in_specs=[vmem] * 6 + [hbm] * 2,
         out_specs=vmem,
         scratch_shapes=[
-            pltpu.VMEM((CHUNKS, pairs * blocks, LANES), F32),
-            pltpu.VMEM((CHUNKS, pairs * blocks, LANES), F32),
+            pltpu.VMEM((nc * pair_dev * blocks, LANES), F32),
+            pltpu.VMEM((CORES, half * blocks, LANES), F32),
             pltpu.VMEM((nv, no), F32),
             pltpu.VMEM((nv, slab), F32),
             pltpu.VMEM((padded, slab), BF16),
             pltpu.VMEM((padded, slab), BF16),
-            pltpu.VMEM((CHUNKS, pairs, blocks * LANES), F32),
-            pltpu.VMEM((pairs, blocks * LANES), F32),
-            pltpu.VMEM((COLUMN_BLOCKS, CORES, PLANE, plane_rows, width), F32),
+            pltpu.VMEM((CORES, half, padded), F32),
+            pltpu.VMEM((half, padded), F32),
+            pltpu.VMEM((CORES, COLUMN_BLOCKS, PLANE, plane_rows, width), F32),
             pltpu.VMEM((COLUMN_BLOCKS, PLANE, plane_rows, width), F32),
             pltpu.VMEM((COLUMN_BLOCKS, PLANE - 1, plane_rows, width), F32),
             pltpu.VMEM((COLUMN_BLOCKS, depth_n, pair_dev, width), F32),
@@ -370,8 +376,8 @@
             pltpu.VMEM((-(-nv // LANES), LANES), F32),
             dma((1,)),
             dma((pieces,)),
-            dma((CHUNKS,)),
-            dma((CHUNKS,)),
+            dma((1,)),
+            dma((CORES,)),
             dma((COLUMN_BLOCKS,)),
             dma((COLUMN_BLOCKS,)),
             dma((COLUMN_BLOCKS, PLANE - 1)),

time: 66.9 us -> 75.6 us (1.13)
  the two profiles are of different devices: /device:TPU:0 before, /device:TPU:1 now
where the time goes in v3:
time: 75.6 us; the launch traced here: 75.4 us
  Pallas kernels  73.9 us (98%)
  other arithmetic  1.48 us (2%)
    pallas_call x1, Pallas kernels, kernel_body(): pl.pallas_call(functools.partial(ladder_kernel, n), out_shape=jax.ShapeDt...  73.9 us

profile of v3, /device:TPU:1, one launch (start us, length us, event | category | flops | bytes accessed | tf_op | source)
XLA Modules:
  0.0 75.4 jit_solution(2361453614032786681)
XLA Ops:
  0.0 73.9 %shard_map.82 = f32[6,2048]{1,0:T(8,128)} custom-call(f32[6,1,32,2000]{3,2,1,0:T(8,128)} %amp_ref.1, s32[192]{0:T(256)} %mirror_ref.1, s32[2,192]{1,0:T(2,128)} %bitcast.9, s32[2,2048]{1,0:T(2,128)} %bitcast.8, f32[250]{0:T(256)} %occ_ref.1, f32[2000]{0:T(1024)} %vir_ref.1, f32[2000,250]{1,0:T(8,128)} %bitcast.7, f32[2000,2048]{1,0:T(8,128)} %bitcast.6), custom_call_target="tpu_custom_call" | custom-call | tf_op jit(solution)/shard_map/pallas_call | solution.py:356
  73.9 1.5 %broadcast_multiply_fusion = f32[6,2048]{1,0:T(8,128)} fusion(f32[6,2048]{1,0:T(8,128)} %shard_map.82), kind=kLoop, calls=%fused_computation | loop fusion | flops 12288 | bytes 98304 | tf_op jit(solution)/shard_map/mul | solution.py:401
